TPU v7x, 32 devices: a whole 2x2x4 slice. The times are simulated.
32 devices in a mesh: ep: 8 (over z, y), sp: 4 (over x, core).
Axes of the slice: x: 2, y: 2, z: 4, core: 2. Of those that a mesh axis runs over, the one named last changes fastest.
Arguments:
- stream: bfloat16 [4096, 4096], P(('ep', 'sp')), may hold values from -30 to 30
- query_base: bfloat16 [4096, 4096], P(('ep', 'sp')), may hold values from -40 to 40
- key_heads: bfloat16 [4096, 1024], P(('ep', 'sp')), may hold values from -6 to 6
- value_heads: bfloat16 [4096, 1024], P(('ep', 'sp')), may hold values from -12 to 12
- attention_gain: bfloat16 [4096], replicated, may hold values from 0.099609375 to 1.8984375
- expert_gain: bfloat16 [4096], replicated, may hold values from 0.099609375 to 1.8984375
- adapter_down: bfloat16 [4096, 128], P('sp'), may hold values from -0.09375 to 0.09375
- adapter_up: bfloat16 [4096, 128], P('sp'), may hold values from -1 to 1
- user_index: int32 [8], P('ep'), may hold values from 0 to 3
- routes: int32 [4096, 2], P('ep'), may hold values from 0 to 7, all different within a row; in each aligned block of 128 rows (0 to 127, 128 to 255, ...) at most 40 rows name the same one
- route_weights: int32 [4096, 2], P(('ep', 'sp')), may hold values from 1 to 4
- gate_weight: bfloat16 [8, 4096, 1536], P('ep', None, 'sp'), may hold values from -0.09375 to 0.09375
- up_weight: bfloat16 [8, 4096, 1536], P('ep', None, 'sp'), may hold values from -0.09375 to 0.09375
- down_weight: bfloat16 [8, 1536, 4096], P('ep', 'sp'), may hold values from -0.15625 to 0.15625
Outputs:
- hidden_state: bfloat16 [4096, 4096], P(('ep', 'sp'))
- moe_out: bfloat16 [4096, 4096], P(('ep', 'sp'))
Inputs may be any that keep to these rules, and one draw needn't show every extreme that they name: `routes`: each row names 2 different experts. In each aligned block of 128 rows (the tokens of one device) no expert is named more than 40 times, and in some block some expert is named exactly 40 times.
All inputs are finite; a program needn't handle non-finite values.
Results may differ from a plain program's by a relative error of at most 0.019.
Values may be sent and summed in bfloat16 or wider, within the bound.
A program may use at most 128 MiB of HBM per device.

v0:
```python
import jax
import jax.numpy as jnp
from jax import lax
from jax.sharding import PartitionSpec as P

D = 4096
HEADS = 32
KV_HEADS = 8
HEAD = 128
RANK = 32


epsilon = 1e-06


def rms_scale(inputs, gain_vec):
    widened = inputs.astype(jnp.float32)
    return (
        widened
        * lax.rsqrt(jnp.mean(widened * widened, axis=-1, keepdims=True) + epsilon)
        * gain_vec.astype(jnp.float32)
    )


def route_slots(block_routes, experts):
    flat_routes = block_routes.reshape(-1)
    matches = (flat_routes[:, None] == jnp.arange(experts, dtype=jnp.int32)[None, :]).astype(
        jnp.int32
    )
    earlier = jnp.cumsum(matches, axis=0) - matches
    return (flat_routes, jnp.sum(earlier * matches, axis=1))


def attention_block(
    stream_rows, base_rows, key_rows, value_rows, user_id, attention_gain, adapter_down, adapter_up
):
    normed = rms_scale(stream_rows, attention_gain).astype(jnp.bfloat16)
    down_cols = lax.dynamic_slice_in_dim(adapter_down, user_id * RANK, RANK, 1)
    up_cols = lax.dynamic_slice_in_dim(adapter_up, user_id * RANK, RANK, 1)
    low_rank = jnp.dot(normed, down_cols, preferred_element_type=jnp.float32).astype(jnp.bfloat16)
    adapter_delta = jnp.dot(low_rank, up_cols.T, preferred_element_type=jnp.float32)
    queries = (base_rows.astype(jnp.float32) + adapter_delta).astype(jnp.bfloat16)
    group_size = HEADS // KV_HEADS
    row_total = queries.shape[0]
    query_heads = queries.reshape(row_total, KV_HEADS, group_size, HEAD)
    key_split = key_rows.reshape(-1, KV_HEADS, HEAD)
    value_split = value_rows.reshape(-1, KV_HEADS, HEAD)
    scores = jnp.einsum(
        "qhgd,khd->hgqk", query_heads, key_split, preferred_element_type=jnp.float32
    ) * HEAD ** (-0.5)
    row_max = jnp.max(scores, axis=-1, keepdims=True)
    exponent = jnp.exp(scores - row_max)
    attn_probs = (exponent / jnp.sum(exponent, axis=-1, keepdims=True)).astype(jnp.bfloat16)
    attended = jnp.einsum(
        "hgqk,khd->qhgd", attn_probs, value_split, preferred_element_type=jnp.float32
    ).reshape(row_total, D)
    return (stream_rows.astype(jnp.float32) + attended).astype(jnp.bfloat16)


def on_device(
    stream,
    query_base,
    key_heads,
    value_heads,
    attention_gain,
    expert_gain,
    adapter_down,
    adapter_up,
    user_index,
    routes,
    route_weights,
    gate_weight,
    up_weight,
    down_weight,
):
    key_all, value_all, down_all, up_all = (
        lax.all_gather(key_heads, "sp", axis=0, tiled=True),
        lax.all_gather(value_heads, "sp", axis=0, tiled=True),
        lax.all_gather(adapter_down, "sp", axis=0, tiled=True),
        lax.all_gather(adapter_up, "sp", axis=0, tiled=True),
    )
    hidden_state = attention_block(
        stream, query_base, key_all, value_all, user_index[0], attention_gain, down_all, up_all
    )
    normed_moe = rms_scale(hidden_state, expert_gain).astype(jnp.bfloat16)
    tokens_dev = stream.shape[0]
    top_count = routes.shape[1]
    model_width = stream.shape[1]
    experts = lax.axis_size("ep")
    capacity = max(2, (5 * tokens_dev * top_count + 4 * experts - 1) // (4 * experts))
    own_routes = lax.dynamic_slice_in_dim(routes, lax.axis_index("sp") * tokens_dev, tokens_dev, 0)
    flat_routes, slot_index = route_slots(own_routes, experts)
    position = flat_routes * capacity + slot_index
    padded = jnp.concatenate([normed_moe, jnp.zeros((1, model_width), jnp.bfloat16)], axis=0)
    token_ids = jnp.arange(tokens_dev * top_count, dtype=jnp.int32) // top_count
    slot_table = jnp.full((experts * capacity,), tokens_dev, jnp.int32).at[position].set(token_ids)
    outgoing = padded[slot_table].reshape(experts, capacity, model_width)
    received = lax.all_to_all(outgoing, "ep", split_axis=0, concat_axis=0, tiled=True)
    arrived = lax.all_gather(received, "sp", axis=0, tiled=True)
    all_rows = arrived.reshape(-1, model_width)
    gate_local = gate_weight[0]
    up_local = up_weight[0]
    down_local = down_weight[0]
    gate_out = jnp.dot(all_rows, gate_local, preferred_element_type=jnp.float32)
    up_out = jnp.dot(all_rows, up_local, preferred_element_type=jnp.float32)
    activated = (jax.nn.silu(gate_out) * up_out).astype(jnp.bfloat16)
    summed = lax.psum_scatter(
        jnp.dot(activated, down_local, preferred_element_type=jnp.float32).astype(jnp.bfloat16),
        "sp",
        scatter_dimension=0,
        tiled=True,
    )
    expert_out = summed.reshape(experts, capacity, model_width)
    returned = lax.all_to_all(expert_out, "ep", split_axis=0, concat_axis=0, tiled=True)
    picked = returned.reshape(experts * capacity, model_width)[position].reshape(
        tokens_dev, top_count, model_width
    )
    route_share = route_weights.astype(jnp.float32)
    route_share = route_share / jnp.sum(route_share, axis=1, keepdims=True)
    moe_out = jnp.sum(picked.astype(jnp.float32) * route_share[:, :, None], axis=1).astype(
        jnp.bfloat16
    )
    return (hidden_state, moe_out)


def solution(mesh):
    in_specs = (
        P(("ep", "sp"), None),
        P(("ep", "sp"), None),
        P(("ep", "sp"), None),
        P(("ep", "sp"), None),
        P(),
        P(),
        P("sp", None),
        P("sp", None),
        P("ep"),
        P("ep", None),
        P(("ep", "sp"), None),
        P("ep", None, "sp"),
        P("ep", None, "sp"),
        P("ep", "sp", None),
    )
    out_specs = (P(("ep", "sp"), None), P(("ep", "sp"), None))
    return jax.shard_map(
        on_device, mesh=mesh, in_specs=in_specs, out_specs=out_specs, check_vma=False
    )
```

profile of v0, /device:TPU:0, one launch (start us, length us, event | category | flops | bytes accessed | tf_op | source)
XLA Modules:
  0.0 456.6 jit_solution(8535833611888024131)
XLA Ops:
  7.2 0.0 copy-start
  7.2 0.0 all-gather.6.cloned.1.call-start
  7.2 0.7 all-gather.6.cloned.1.call-update
  7.9 0.0 all-gather.8.cloned.1.call-start
  8.0 0.7 all-gather.8.cloned.1.call-update
  8.7 0.0 all-gather.10.cloned.1.call-start
  8.7 1.8 copy.29
  10.5 0.0 all-gather.10.cloned.1.call-update
  10.5 0.0 all-gather.12.cloned.1.call-start
  10.6 0.5 all-gather.12.cloned.1.call-update
  11.1 0.0 all-gather.14.cloned.1.call-start
  11.2 0.7 broadcast_multiply_fusion
  11.9 0.1 copy.35
  12.0 0.1 eq.29
  12.1 0.1 eq.25
  12.9 0.6 reduce-window.6
  13.5 0.2 slice_reduce_fusion
  13.8 0.1 copy.34
  13.9 0.1 mul.109
  14.0 0.1 fusion.47
  14.1 1.4 scatter_custom_fusion
  15.6 0.7 convert_element_type.61
  16.3 1.5 fusion.21
  17.8 0.7 convert_element_type.68
  18.5 10.5 %all-gather.6.cloned.1.call-done = bf16[4096,128]{1,0:T(8,128)(2,1)} async-done(((bf16[1024,128]{1,0:T(8,128)(2,1)}), bf16[4096,128]{1,0:T(8,128)(2,1)}) %all-gather.6.cloned.1.call-update) | async-done | bytes 1048592 | tf_op jit(solution)/shard_map/all_gather | solution.py:79
  29.0 18.3 %all-gather.8.cloned.1.call-done = bf16[4096,128]{1,0:T(8,128)(2,1)} async-done(((bf16[1024,128]{1,0:T(8,128)(2,1)}), bf16[4096,128]{1,0:T(8,128)(2,1)}) %all-gather.8.cloned.1.call-update) | async-done | bytes 1048592 | tf_op jit(solution)/shard_map/all_gather | solution.py:80
  47.3 4.9 %fusion.6 = bf16[128,4096]{1,0:T(8,128)(2,1)} fusion(bf16[128,4096]{1,0:T(8,128)(2,1)} %param.15, bf16[128,4096]{1,0:T(8,128)(2,1)} %param.14, bf16[4096,128]{1,0:T(8,128)(2,1)} %all-gather.8.cloned.1.call-done, s32[]{:T(128)S(6)} %select_n.26, bf16[4096,128]{1,0:T(8,128)(2,1)} %all-gather.6.cloned.1.call-done, f32[4096]{0:T(1024)S(1)} %convert_element_type.61, ...), kind=kOutput, calls=%fused_computation.12 | convolution fusion | flops 70782976 | bytes 5260800 | tf_op jit(solution)/shard_map/dot_general | solution.py:41
  52.2 2.6 reshape.101
  54.8 11.0 %all-gather.10.cloned.1.call-done = bf16[512,1024]{0,1:T(8,128)(2,1)} async-done(((bf16[128,1024]{0,1:T(8,128)(2,1)}), bf16[512,1024]{0,1:T(8,128)(2,1)}) %all-gather.10.cloned.1.call-update) | async-done | bytes 1048592 | tf_op jit(solution)/shard_map/all_gather | solution.py:77
  65.8 2.8 fusion.32
  68.6 0.0 copy-start.1
  68.6 3.2 copy-done.1
  71.8 2.4 fusion.59
  74.2 9.7 %all-gather.12.cloned.1.call-done = bf16[512,1024]{1,0:T(8,128)(2,1)} async-done(((bf16[128,1024]{1,0:T(8,128)(2,1)}), bf16[512,1024]{1,0:T(8,128)(2,1)}) %all-gather.12.cloned.1.call-update) | async-done | bytes 1048592 | tf_op jit(solution)/shard_map/all_gather | solution.py:78
  84.0 2.3 copy.32
  86.2 12.1 %fusion.8 = f32[8,4,128,128]{2,3,1,0:T(8,128)} fusion(bf16[512,8,128,1]{0,2,3,1:T(8,128)(2,1)} %bitcast.68, f32[8,4,128]{2,1,0:T(4,128)S(1)} %fusion.59, f32[8,128,4,512]{3,1,2,0:T(8,128)} %copy-done.1), kind=kOutput, calls=%fused_computation.15 | convolution fusion | flops 547361280 | bytes 11550720 | tf_op jit(solution)/shard_map/hgqk,khd->qhgd/dot_general | solution.py:54
  98.4 2.9 copy.33
  101.3 2.3 fusion.18
  103.5 0.0 copy-start.2
  103.6 1.0 copy-done.2
  104.5 0.3 fusion.20
  104.9 1.1 concatenate.3
  106.0 9.5 %gather_fusion = bf16[320,4096]{1,0:T(8,128)(2,1)} fusion(bf16[129,4096]{1,0:T(8,128)(2,1)} %concatenate.3, s32[1024]{0:T(1024)S(1)} %pad_clamp_fusion.1), kind=kCustom, calls=%fused_computation | custom fusion | bytes 5244160 | tf_op jit(solution)/shard_map/gather | solution.py:97
  115.5 65.4 %all_to_all.10 = bf16[8,40,4096]{2,1,0:T(8,128)(2,1)} all-to-all(bf16[8,40,4096]{2,1,0:T(8,128)(2,1)} %bitcast.64), channel_id=1, replica_groups=mesh['ep'=8,'sp'=4] {'ep'}, dimensions={0} | all-to-all | bytes 5242880 | tf_op jit(solution)/shard_map/all_to_all | solution.py:98
  180.9 0.0 all-gather.14.cloned.1.call-update
  180.9 0.0 reduce-scatter.2.cloned.1.call-start
  181.0 68.4 %all-gather.14.cloned.1.call-done = bf16[32,40,4096]{2,1,0:T(8,128)(2,1)} async-done(((bf16[8,40,4096]{2,1,0:T(8,128)(2,1)}), bf16[32,40,4096]{2,1,0:T(8,128)(2,1)}) %all-gather.14.cloned.1.call-update) | async-done | bytes 10485776 | tf_op jit(solution)/shard_map/all_gather | solution.py:99
  249.4 10.2 %fusion.11 = f32[1280,384]{1,0:T(8,128)} fusion(bf16[1280,4096]{1,0:T(8,128)(2,1)} %bitcast.72, bf16[1,4096,384]{2,1,0:T(8,128)(2,1)} %param.25), kind=kOutput, calls=%fused_computation.19 | convolution fusion | flops 4026531840 | bytes 15597568 | tf_op jit(solution)/shard_map/dot_general | solution.py:104
  259.6 0.0 copy-done
  259.6 17.2 %convolution_convert_fusion = bf16[1280,4096]{1,0:T(8,128)(2,1)} fusion(bf16[1,384,4096]{2,1,0:T(8,128)(2,1)S(1)} %copy-done, bf16[1280,4096]{1,0:T(8,128)(2,1)} %bitcast.73, bf16[1,4096,384]{2,1,0:T(8,128)(2,1)} %param.26, f32[1280,384]{1,0:T(8,128)} %fusion.11), kind=kOutput, calls=%fused_computation.4 | convolution fusion | flops 8061255680 | bytes 29229056 | tf_op jit(solution)/shard_map/dot_general | solution.py:108
  276.8 0.0 reduce-scatter.2.cloned.1.call-update
  276.8 0.0 copy-start.3
  276.8 85.5 %reduce-scatter.2.cloned.1.call-done = bf16[320,4096]{1,0:T(8,128)(2,1)} async-done(((bf16[1280,4096]{1,0:T(8,128)(2,1)}), bf16[320,4096]{1,0:T(8,128)(2,1)}) %reduce-scatter.2.cloned.1.call-update) | async-done | bytes 2621456 | tf_op jit(solution)/shard_map/reduce_scatter | solution.py:107
  362.3 5.5 %all-to-all-start.1 = ((bf16[8,40,4096]{2,1,0:T(8,128)(2,1)}), bf16[8,40,4096]{2,1,0:T(8,128)(2,1)}, u32[]{:S(2)}, u32[]{:S(2)}) async-start(bf16[8,40,4096]{2,1,0:T(8,128)(2,1)} %bitcast.65), calls=%async_computation.2 | async-start | bytes 5242880 | tf_op jit(solution)/shard_map/all_to_all | solution.py:114
  367.8 0.0 copy-done.3
  367.8 0.1 copy.37
  368.0 59.4 %all-to-all-done.1 = bf16[8,40,4096]{2,1,0:T(8,128)(2,1)} async-done(((bf16[8,40,4096]{2,1,0:T(8,128)(2,1)}), bf16[8,40,4096]{2,1,0:T(8,128)(2,1)}, u32[]{:S(2)}, u32[]{:S(2)}) %all-to-all-start.1) | async-done | bytes 2621472 | tf_op jit(solution)/shard_map/all_to_all | solution.py:114
  427.4 7.3 %gather_fusion.1 = bf16[256,4096]{1,0:T(8,128)(2,1)} fusion(bf16[320,4096]{1,0:T(8,128)(2,1)} %bitcast.19, s32[1024]{0:T(1024)S(1)} %pad_clamp_fusion), kind=kCustom, calls=%fused_computation.1 | custom fusion | bytes 4195328 | tf_op jit(solution)/shard_map/gather | solution.py:115
  434.7 5.4 %reshape.110 = f32[128,2,4096]{2,1,0:T(2,128)} reshape(bf16[256,4096]{1,0:T(8,128)(2,1)} %gather_fusion.1) | data formatting | bytes 6291456 | tf_op jit(solution)/shard_map/convert_element_type | solution.py:120
  440.1 9.6 %multiply_reduce_fusion = bf16[128,4096]{1,0:T(8,128)(2,1)} fusion(f32[128,2,4096]{2,1,0:T(2,128)} %reshape.110, f32[128,2]{1,0:T(8,128)S(1)} %copy.37), kind=kLoop, calls=%fused_computation.13 | loop fusion | flops 1572864 | bytes 5243904 | tf_op jit(solution)/shard_map/reduce_sum | solution.py:120
  (12 shorter events, 0.1 us)
Async XLA Ops:
  7.2 252.4 %copy-start = (bf16[1,384,4096]{2,1,0:T(8,128)(2,1)S(1)}, bf16[1,384,4096]{2,1,0:T(8,128)(2,1)}, u32[]{:S(2)}) copy-start(bf16[1,384,4096]{2,1,0:T(8,128)(2,1)} %param.27) | copy-start | bytes 9437188
  7.2 21.8 %all-gather.6.cloned.1.call-start = ((), (), s32[]{:S(2)}) async-start(), calls=%async_computation.3 | async-start | bytes 1310720 | tf_op jit(solution)/shard_map/all_gather | solution.py:79
  7.9 39.4 %all-gather.8.cloned.1.call-start = ((), (), s32[]{:S(2)}) async-start(), calls=%async_computation.4 | async-start | bytes 1310720 | tf_op jit(solution)/shard_map/all_gather | solution.py:80
  8.7 57.1 %all-gather.10.cloned.1.call-start = ((), (), s32[]{:S(2)}) async-start(), calls=%async_computation.5 | async-start | bytes 1310720 | tf_op jit(solution)/shard_map/all_gather | solution.py:77
  10.5 73.4 %all-gather.12.cloned.1.call-start = ((), (), s32[]{:S(2)}) async-start(), calls=%async_computation.6 | async-start | bytes 1310720 | tf_op jit(solution)/shard_map/all_gather | solution.py:78
  11.1 238.3 %all-gather.14.cloned.1.call-start = ((), (), s32[]{:S(2)}) async-start(), calls=%async_computation.7 | async-start | bytes 13107200 | tf_op jit(solution)/shard_map/all_gather | solution.py:99
  68.6 3.2 copy-start.1
  103.5 1.0 copy-start.2
  180.9 181.3 %reduce-scatter.2.cloned.1.call-start = ((), (), s32[]{:S(2)}) async-start(), calls=%async_computation.8 | async-start | bytes 13107200 | tf_op jit(solution)/shard_map/reduce_scatter | solution.py:107
  276.8 91.0 %copy-start.3 = (s32[128,2]{0,1:T(2,128)S(1)}, s32[128,2]{0,1:T(2,128)}, u32[]{:S(2)}) copy-start(s32[128,2]{0,1:T(2,128)} %param.24) | copy-start | bytes 3076
  362.3 65.1 %all-to-all-start.1 = ((bf16[8,40,4096]{2,1,0:T(8,128)(2,1)}), bf16[8,40,4096]{2,1,0:T(8,128)(2,1)}, u32[]{:S(2)}, u32[]{:S(2)}) async-start(bf16[8,40,4096]{2,1,0:T(8,128)(2,1)} %bitcast.65), calls=%async_computation.2 | async-start | bytes 5242880 | tf_op jit(solution)/shard_map/all_to_all | solution.py:114
Sparse Core Ops, SparseCore 0:
  9.6 19.4 all-gather.5
  30.6 16.7 all-gather.7
  48.9 16.8 all-gather.9
  67.2 16.7 all-gather.11
  181.1 68.3 all-gather.13
  276.9 85.2 reduce-scatter.1
where the time goes:
time: 457 us
  waiting for transfers between devices  265 us (58%)
  blocking collectives  65.4 us (14%)
  matrix products  47.2 us (10%)
  local copies, waits for them, and re-layouts  39.5 us (9%)
  other arithmetic  19 us (4%)
  between operations  14.9 us (3%)
  starting transfers between devices  5.75 us (1%)
    reduce_scatter x1, waiting for transfers between devices, on_device(): lax.psum_scatter(jnp.dot(activated, down_local, preferred_element_type=jn...  85.5 us
    all_gather x1, waiting for transfers between devices, on_device(): arrived = lax.all_gather(received, 'sp', axis=0, tiled=True)  68.4 us
    all_to_all x1, blocking collectives, on_device(): lax.all_to_all(outgoing, 'ep', split_axis=0, concat_axis=0, tiled=True)  65.4 us
    all_to_all x1, waiting for transfers between devices, on_device(): lax.all_to_all(expert_out, 'ep', split_axis=0, concat_axis=0, tiled=True)  59.4 us
    all_gather x1, waiting for transfers between devices, on_device(): lax.all_gather(adapter_up, 'sp', axis=0, tiled=True)  18.3 us
    dot_general x1, matrix products, on_device(): jnp.dot(activated, down_local, preferred_element_type=jnp.float32)  17.2 us
    dot_general x1, matrix products, attention_block(): jnp.einsum('hgqk,khd->qhgd', attn_probs, value_split, preferred_element_t...  12.1 us
    all_gather x1, waiting for transfers between devices, on_device(): lax.all_gather(key_heads, 'sp', axis=0, tiled=True)  11 us
  transfers between devices with their start and end apart: 7, of which 7 were waited for; matrix products, arithmetic and copies ran while one was open for 5% of the time, Pallas kernels for 0%

commit v1 on v0

v1 whole, which is shorter than its diff:
```python
import jax
import jax.numpy as jnp
from jax import lax
from jax.experimental import pallas as pl
from jax.experimental.pallas import tpu as pltpu
from jax.sharding import PartitionSpec as P

D = 4096
HEADS = 32
KV_HEADS = 8
HEAD = 128
RANK = 32


epsilon = 1e-06


def rms_scale(inputs, gain_vec):
    widened = inputs.astype(jnp.float32)
    return (
        widened
        * lax.rsqrt(jnp.mean(widened * widened, axis=-1, keepdims=True) + epsilon)
        * gain_vec.astype(jnp.float32)
    )


def route_slots(block_routes, experts):
    flat_routes = block_routes.reshape(-1)
    matches = (flat_routes[:, None] == jnp.arange(experts, dtype=jnp.int32)[None, :]).astype(
        jnp.int32
    )
    earlier = jnp.cumsum(matches, axis=0) - matches
    return (flat_routes, jnp.sum(earlier * matches, axis=1))


def attention_block(
    stream_rows, base_rows, key_rows, value_rows, attention_gain, down_cols, up_cols
):
    normed = rms_scale(stream_rows, attention_gain).astype(jnp.bfloat16)
    low_rank = lax.dot_general(
        normed, down_cols, (((1,), (1,)), ((), ())), preferred_element_type=jnp.float32
    ).astype(jnp.bfloat16)
    adapter_delta = jnp.dot(low_rank, up_cols, preferred_element_type=jnp.float32)
    queries = (base_rows.astype(jnp.float32) + adapter_delta).astype(jnp.bfloat16)
    group_size = HEADS // KV_HEADS
    row_total = queries.shape[0]
    query_heads = queries.reshape(row_total, KV_HEADS, group_size, HEAD)
    key_split = key_rows.reshape(-1, KV_HEADS, HEAD)
    value_split = value_rows.reshape(-1, KV_HEADS, HEAD)
    scores = jnp.einsum(
        "qhgd,khd->hgqk", query_heads, key_split, preferred_element_type=jnp.float32
    ) * HEAD ** (-0.5)
    row_max = jnp.max(scores, axis=-1, keepdims=True)
    exponent = jnp.exp(scores - row_max)
    attn_probs = (exponent / jnp.sum(exponent, axis=-1, keepdims=True)).astype(jnp.bfloat16)
    attended = jnp.einsum(
        "hgqk,khd->qhgd", attn_probs, value_split, preferred_element_type=jnp.float32
    ).reshape(row_total, D)
    return (stream_rows.astype(jnp.float32) + attended).astype(jnp.bfloat16)


STEPS = 8


def peer_mask(step):
    return (step * 2) % STEPS + step // 4


def xor3(a, b):
    total = 0
    for place in (1, 2, 4):
        abit, bbit = (a // place) % 2, (b // place) % 2
        total = total + place * (abit + bbit - 2 * abit * bbit)
    return total


def expert_kernel(
    outgoing,
    gate_hbm,
    up_hbm,
    down_hbm,
    returned,
    arrived,
    part,
    from_core,
    from_x,
    rows_in,
    gate_w,
    up_w,
    down_w,
    weight_sem,
    send_sem,
    recv_sem,
):
    me, sp = lax.axis_index("ep"), lax.axis_index("sp")
    xpos, core = sp // 2, sp % 2
    core_dev, x_dev = xpos * 2 + (1 - core), (1 - xpos) * 2 + core
    q_me, q_core = core * 2 + xpos, (1 - core) * 2 + xpos
    q_x, q_diag = core * 2 + (1 - xpos), (1 - core) * 2 + (1 - xpos)
    cap, width = outgoing.shape[1], outgoing.shape[2]
    Z, C1, X, C2, RC, RX, FIN = range(7)

    def remote(kind, step, src, dst, ep_dev, sp_dev):
        return pltpu.make_async_remote_copy(
            src_ref=src,
            dst_ref=dst,
            send_sem=send_sem.at[kind, step],
            recv_sem=recv_sem.at[kind, step],
            device_id=(ep_dev, sp_dev),
            device_id_type=pl.DeviceIdType.MESH,
        )

    def peer(step):
        return xor3(me, peer_mask(step))

    def z_send(k):
        return remote(Z, k, outgoing.at[k], arrived.at[k, q_me], peer(k), sp)

    def core_send(k):
        return remote(C1, k, arrived.at[k, q_me], arrived.at[k, q_me], me, core_dev)

    def x_send(k):
        return remote(X, k, arrived.at[k, q_me], arrived.at[k, q_me], me, x_dev)

    def core_forward(k):
        return remote(C2, k, arrived.at[k, q_x], arrived.at[k, q_x], me, core_dev)

    def part_send(k):
        return remote(RC, k, part.at[k, pl.ds((1 - core) * 2, 2)], from_core.at[k], me, core_dev)

    def x_part_send(k):
        return remote(RX, k, part.at[k, q_x], from_x.at[k], me, x_dev)

    def final_send(k):
        return remote(FIN, k, part.at[k, q_me], returned.at[k], peer(k), sp)

    weights = [
        pltpu.make_async_copy(src, dst, weight_sem.at[n])
        for n, (src, dst) in enumerate(((gate_hbm, gate_w), (up_hbm, up_w), (down_hbm, down_w)))
    ]
    for copy in weights:
        copy.start()
    barrier = pltpu.get_barrier_semaphore()
    for step in range(1, STEPS):
        pl.semaphore_signal(
            barrier, inc=1, device_id=(peer(step), sp), device_id_type=pl.DeviceIdType.MESH
        )
    for near in (core_dev, x_dev):
        pl.semaphore_signal(
            barrier, inc=1, device_id=(me, near), device_id_type=pl.DeviceIdType.MESH
        )
    pl.semaphore_wait(barrier, STEPS + 1)

    for step in range(1, STEPS):
        z_send(step).start()
    arrived[0, q_me] = outgoing[0]

    def compute(k):
        chunk = 512
        for col in range(0, width, chunk):
            cols = slice(col, col + chunk)
            rows_in[:, cols] = jnp.concatenate(
                [arrived[k, q, :, cols].astype(jnp.float32) for q in range(4)], axis=0
            ).astype(jnp.bfloat16)
        rows = rows_in[...]
        gate = jnp.dot(rows, gate_w[...], preferred_element_type=jnp.float32)
        up = jnp.dot(rows, up_w[...], preferred_element_type=jnp.float32)
        act = (gate / (1.0 + jnp.exp(-gate)) * up).astype(jnp.bfloat16)
        for col in range(0, width, chunk):
            cols = slice(col, col + chunk)
            out = jnp.dot(act, down_w[:, cols], preferred_element_type=jnp.float32)
            for q in range(4):
                part[k, q, :, cols] = out[q * cap : (q + 1) * cap].astype(jnp.bfloat16)

    def body(t, carry):
        @pl.when(t < STEPS)
        def _():
            @pl.when(t > 0)
            def _():
                remote(Z, t, outgoing.at[t], arrived.at[t, q_me], peer(t), sp).wait_recv()

            x_send(t).start()
            core_send(t).start()

        @pl.when((t >= 1) & (t < STEPS + 1))
        def _():
            k = t - 1
            remote(X, k, arrived.at[k, q_x], arrived.at[k, q_x], me, x_dev).wait_recv()
            core_forward(k).start()

        @pl.when(t == 2)
        def _():
            for copy in weights:
                copy.wait()

        @pl.when((t >= 2) & (t < STEPS + 2))
        def _():
            k = t - 2
            remote(C1, k, arrived.at[k, q_core], arrived.at[k, q_core], me, core_dev).wait_recv()
            remote(C2, k, arrived.at[k, q_diag], arrived.at[k, q_diag], me, core_dev).wait_recv()
            compute(k)
            part_send(k).start()

        @pl.when((t >= 3) & (t < STEPS + 3))
        def _():
            k = t - 3
            part_send(k).wait_recv()
            part[k, q_x] = (
                part[k, q_x].astype(jnp.float32)
                + from_core[k, 1 - xpos].astype(jnp.float32)
            ).astype(jnp.bfloat16)
            x_part_send(k).start()

        @pl.when(t >= 4)
        def _():
            k = t - 4
            x_part_send(k).wait_recv()
            part[k, q_me] = (
                part[k, q_me].astype(jnp.float32)
                + from_core[k, xpos].astype(jnp.float32)
                + from_x[k].astype(jnp.float32)
            ).astype(jnp.bfloat16)

            @pl.when(k > 0)
            def _():
                final_send(k).start()

        return carry

    lax.fori_loop(0, STEPS + 4, body, 0)
    returned[0] = part[0, q_me]
    for k in range(STEPS):
        if k > 0:
            z_send(k).wait_send()
            final_send(k).wait()
        for copy in (core_send, x_send, core_forward, part_send, x_part_send):
            copy(k).wait_send()


def expert_exchange(outgoing, gate_local, up_local, down_local):
    steps, cap, width = outgoing.shape
    hidden = gate_local.shape[1]
    rows = 4 * steps * cap
    dma = pltpu.SemaphoreType.DMA
    return pl.pallas_call(
        expert_kernel,
        out_shape=jax.ShapeDtypeStruct(outgoing.shape, jnp.bfloat16),
        in_specs=[pl.BlockSpec(memory_space=pltpu.VMEM)] + [pl.BlockSpec(memory_space=pl.ANY)] * 3,
        out_specs=pl.BlockSpec(memory_space=pltpu.VMEM),
        scratch_shapes=[
            pltpu.VMEM((steps, 4, cap, width), jnp.bfloat16),
            pltpu.VMEM((steps, 4, cap, width), jnp.bfloat16),
            pltpu.VMEM((steps, 2, cap, width), jnp.bfloat16),
            pltpu.VMEM((steps, cap, width), jnp.bfloat16),
            pltpu.VMEM((4 * cap, width), jnp.bfloat16),
            pltpu.VMEM(gate_local.shape, jnp.bfloat16),
            pltpu.VMEM(up_local.shape, jnp.bfloat16),
            pltpu.VMEM(down_local.shape, jnp.bfloat16),
            dma((3,)),
            dma((7, steps)),
            dma((7, steps)),
        ],
        compiler_params=pltpu.CompilerParams(
            collective_id=0, has_side_effects=True, vmem_limit_bytes=60 * 1024 * 1024
        ),
        cost_estimate=pl.CostEstimate(
            flops=6 * rows * width * hidden, bytes_accessed=8 * rows * width, transcendentals=0
        ),
    )(outgoing, gate_local, up_local, down_local)


def expert_collectives(outgoing, gate_local, up_local, down_local):
    experts, capacity, model_width = outgoing.shape
    received = lax.all_to_all(outgoing, "ep", split_axis=0, concat_axis=0, tiled=True)
    all_rows = lax.all_gather(received, "sp", axis=0, tiled=True).reshape(-1, model_width)
    gate_out = jnp.dot(all_rows, gate_local, preferred_element_type=jnp.float32)
    up_out = jnp.dot(all_rows, up_local, preferred_element_type=jnp.float32)
    activated = (jax.nn.silu(gate_out) * up_out).astype(jnp.bfloat16)
    summed = lax.psum_scatter(
        jnp.dot(activated, down_local, preferred_element_type=jnp.float32).astype(jnp.bfloat16),
        "sp",
        scatter_dimension=0,
        tiled=True,
    )
    expert_out = summed.reshape(experts, capacity, model_width)
    return lax.all_to_all(expert_out, "ep", split_axis=0, concat_axis=0, tiled=True)


def on_device(
    stream,
    query_base,
    key_heads,
    value_heads,
    attention_gain,
    expert_gain,
    adapter_down,
    adapter_up,
    user_index,
    routes,
    route_weights,
    gate_weight,
    up_weight,
    down_weight,
):
    user_id = user_index[0]
    tokens_dev, model_width = stream.shape
    down_cols = lax.dynamic_slice_in_dim(adapter_down, user_id * RANK, RANK, 1).T
    up_cols = lax.dynamic_slice_in_dim(adapter_up, user_id * RANK, RANK, 1).T
    shared = jnp.concatenate([key_heads, value_heads, down_cols, up_cols], axis=0)
    shared = lax.all_gather(shared, "sp", axis=0, tiled=False)
    key_all = shared[:, :tokens_dev].reshape(-1, key_heads.shape[1])
    value_all = shared[:, tokens_dev : 2 * tokens_dev].reshape(-1, value_heads.shape[1])
    adapters = shared[:, 2 * tokens_dev :].transpose(1, 0, 2).reshape(2 * RANK, model_width)
    hidden_state = attention_block(
        stream, query_base, key_all, value_all, attention_gain, adapters[:RANK], adapters[RANK:]
    )
    normed_moe = rms_scale(hidden_state, expert_gain).astype(jnp.bfloat16)
    top_count = routes.shape[1]
    experts = lax.axis_size("ep")
    capacity = max(2, (5 * tokens_dev * top_count + 4 * experts - 1) // (4 * experts))
    own_routes = lax.dynamic_slice_in_dim(routes, lax.axis_index("sp") * tokens_dev, tokens_dev, 0)
    in_kernel = experts == STEPS and capacity % 8 == 0 and lax.axis_size("sp") == 4
    flat_routes, slot_index = route_slots(own_routes, experts)
    if in_kernel:
        mask = flat_routes ^ lax.axis_index("ep")
        flat_routes = mask // 2 + (mask % 2) * 4
    position = (flat_routes * capacity + slot_index).reshape(tokens_dev, top_count)
    slots = jnp.arange(experts * capacity, dtype=jnp.int32)
    chosen = position[:, :, None] == slots
    placed = jnp.any(chosen, axis=1).astype(jnp.bfloat16)
    outgoing = (
        lax.dot_general(
            placed, normed_moe, (((0,), (0,)), ((), ())), preferred_element_type=jnp.float32
        )
        .astype(jnp.bfloat16)
        .reshape(experts, capacity, model_width)
    )
    exchange = expert_exchange if in_kernel else expert_collectives
    returned = exchange(outgoing, gate_weight[0], up_weight[0], down_weight[0])
    returned = returned.reshape(experts * capacity, model_width)
    route_share = route_weights.astype(jnp.float32)
    route_share = route_share / jnp.sum(route_share, axis=1, keepdims=True)
    moe_out = sum(
        jnp.dot(
            chosen[:, k].astype(jnp.bfloat16), returned, preferred_element_type=jnp.float32
        )
        * route_share[:, k : k + 1]
        for k in range(top_count)
    ).astype(jnp.bfloat16)
    return (hidden_state, moe_out)


def solution(mesh):
    in_specs = (
        P(("ep", "sp"), None),
        P(("ep", "sp"), None),
        P(("ep", "sp"), None),
        P(("ep", "sp"), None),
        P(),
        P(),
        P("sp", None),
        P("sp", None),
        P("ep"),
        P("ep", None),
        P(("ep", "sp"), None),
        P("ep", None, "sp"),
        P("ep", None, "sp"),
        P("ep", "sp", None),
    )
    out_specs = (P(("ep", "sp"), None), P(("ep", "sp"), None))
    return jax.shard_map(
        on_device, mesh=mesh, in_specs=in_specs, out_specs=out_specs, check_vma=False
    )
```

time: 457 us -> 232 us (0.51)
  waiting for transfers between devices: 265 us -> 25.2 us
  Pallas kernels: 0 us -> 147 us
  blocking collectives: 65.4 us -> 0 us
  matrix products: 47.2 us -> 21.3 us
  local copies, waits for them, and re-layouts: 39.5 us -> 14.1 us
  other arithmetic: 19 us -> 6.85 us
  starting transfers between devices: 5.75 us -> 0.04 us
    pallas_call x0 -> x1, Pallas kernels: none -> 147 us  [expert_exchange(): pl.pallas_call(expert_kernel, out_shape=jax.ShapeDtypeStruct(outgoing.sha...]
    all_gather x5 -> x1, waiting for transfers between devices: 118 us -> 25.2 us  [on_device(): shared = lax.all_gather(shared, 'sp', axis=0, tiled=False)]
    reduce_scatter x1 -> x0, waiting for transfers between devices: 85.5 us -> none  [on_device(): lax.psum_scatter(jnp.dot(activated, down_local, preferred_element_type=jn...]
    all_to_all x1 -> x0, blocking collectives: 65.4 us -> none  [on_device(): lax.all_to_all(outgoing, 'ep', split_axis=0, concat_axis=0, tiled=True)]
    all_to_all x1 -> x0, waiting for transfers between devices: 59.4 us -> none  [on_device(): lax.all_to_all(expert_out, 'ep', split_axis=0, concat_axis=0, tiled=True)]
    dot_general x3 -> x4, matrix products: 32.2 us -> 10.2 us  [the longest x2 4.4 us: on_device(): jnp.dot(chosen[:, k].astype(jnp.bfloat16), returned, preferred_element_ty...]
    gather x2 -> x0, local copies, waits for them, and re-layouts: 16.7 us -> none  [the longest x1 9.45 us: on_device(): outgoing = padded[slot_table].reshape(experts, capacity, model_width)]
    reduce_sum x1 -> x0, other arithmetic: 9.64 us -> none  [on_device(): jnp.sum(picked.astype(jnp.float32) * route_share[:, :, None], axis=1)]
  transfers between devices with their start and end apart: 7 -> 1, of which waited for: 7 -> 1; matrix products, arithmetic and copies ran while one was open for 5% -> 1% of each run, Pallas kernels for 0% -> 0%
where the time goes in v1:
time: 232 us; the launch traced here: 229 us
  Pallas kernels  147 us (63%)
  waiting for transfers between devices  25.2 us (11%)
  matrix products  21.3 us (9%)
  between operations  15 us (6%)
  local copies, waits for them, and re-layouts  14.1 us (6%)
  other arithmetic  6.85 us (3%)
    pallas_call x1, Pallas kernels, expert_exchange(): pl.pallas_call(expert_kernel, out_shape=jax.ShapeDtypeStruct(outgoing.sha...  147 us
    all_gather x1, waiting for transfers between devices, on_device(): shared = lax.all_gather(shared, 'sp', axis=0, tiled=False)  25.2 us
    dot_general x1, matrix products, attention_block(): jnp.einsum('hgqk,khd->qhgd', attn_probs, value_split, preferred_element_t...  9.83 us
  transfers between devices with their start and end apart: 1, of which 1 were waited for; matrix products, arithmetic and copies ran while one was open for 1% of the time, Pallas kernels for 0%

profile of v1, /device:TPU:0, one launch (start us, length us, event | category | flops | bytes accessed | tf_op | source)
XLA Modules:
  0.0 229.2 jit_solution(4483011275140188672)
XLA Ops:
  7.2 0.0 copy-start.8
  7.2 0.0 copy-start.5
  7.2 0.0 copy-start.6
  7.2 0.0 copy-start.7
  7.2 0.0 copy-start.2
  7.2 0.0 all-gather.3.cloned.1.call-start
  8.0 1.2 dynamic-slice_bitcast_fusion
  9.2 0.1 copy.43
  9.4 0.1 copy.44
  9.5 1.9 pad_maximum_fusion
  11.4 0.0 all-gather.3.cloned.1.call-update
  11.4 0.0 copy-done.8
  11.5 0.1 copy.51
  11.6 0.1 eq.44
  11.7 0.1 eq.40
  11.8 0.0 copy-done.5
  11.9 0.6 convert_element_type.55
  12.5 0.6 reduce-window.6
  13.0 0.2 slice_reduce_fusion
  13.3 0.1 fusion.36
  13.4 0.1 reduce_sum.50
  13.5 0.1 copy.53
  13.6 0.0 copy-done.6
  13.6 0.0 copy-done.7
  13.6 0.0 copy-done.2
  13.7 0.3 fusion.14
  13.9 0.6 add_rsqrt_fusion.1
  14.6 0.1 iota_compare_fusion
  14.6 25.2 %all-gather.3.cloned.1.call-done = bf16[1280,1024]{1,0:T(8,128)(2,1)} async-done(((bf16[320,1024]{1,0:T(8,128)(2,1)}), bf16[1280,1024]{1,0:T(8,128)(2,1)}) %all-gather.3.cloned.1.call-update) | async-done | bytes 2621456 | tf_op jit(solution)/shard_map/all_gather | solution.py:310
  39.8 1.1 slice.54
  40.9 2.8 %fusion.46 = (bf16[4,128,1024]{2,1,0:T(8,128)(2,1)S(1)}, bf16[4,128,1024]{2,1,0:T(8,128)(2,1)}) fusion(bf16[4,320,1024]{2,1,0:T(8,128)(2,1)} %bitcast.80), kind=kLoop, calls=%fused_computation.70 | loop fusion | bytes 4194304 | tf_op jit(solution)/shard_map/slice | solution.py:312
  43.7 0.0 copy-start.4
  43.7 0.4 copy.74
  44.1 0.2 fusion.47
  44.3 0.1 copy.65
  44.4 0.8 copy.66
  45.1 0.0 copy-done.4
  45.2 3.4 %fusion.7 = bf16[128,4096]{1,0:T(8,128)(2,1)} fusion(bf16[32,4096]{1,0:T(8,128)(2,1)} %bitcast.87, bf16[128,4096]{1,0:T(8,128)(2,1)S(1)} %copy-done.4, bf16[32,4096]{1,0:T(8,128)(2,1)S(1)} %bitcast.86, bf16[128,4096]{1,0:T(8,128)(2,1)S(1)} %copy-done.2, f32[4096]{0:T(1024)} %convert_element_type.55, f32[128]{0:T(128)} %add_rsqrt_fusion.1), kind=kOutput, calls=%fused_computation.12 | convolution fusion | flops 70782976 | bytes 3686912 | tf_op jit(solution)/shard_map/dot_general | solution.py:43
  48.5 1.8 reshape.95
  50.3 1.5 copy.64
  51.8 1.3 fusion.21
  53.1 0.0 copy-start
  53.1 2.2 fusion.48
  55.4 1.0 copy-done
  56.3 0.3 copy.63
  56.6 9.8 %fusion.10 = f32[8,128,4,128]{3,1,2,0:T(8,128)} fusion(f32[8,4,128]{2,1,0:T(4,128)S(1)} %fusion.48, bf16[512,8,128,1]{2,1,0,3:T(8,128)(2,1)S(1)} %bitcast.83, f32[8,512,128,4]{2,1,3,0:T(8,128)} %copy-done), kind=kOutput, calls=%fused_computation.15 | convolution fusion | flops 547361280 | bytes 11550720 | tf_op jit(solution)/shard_map/hgqk,khd->qhgd/dot_general | solution.py:56
  66.4 1.9 copy.50
  68.4 0.4 fusion.11
  68.8 0.0 copy-start.3
  68.8 2.4 %convolution_convert_fusion = bf16[320,4096]{1,0:T(8,128)(2,1)} fusion(pred[128,320]{0,1:T(8,128)(4,1)S(1)} %get-tuple-element.11, bf16[128,4096]{1,0:T(8,128)(2,1)S(1)} %get-tuple-element.3, f32[4096]{0:T(1024)S(1)} %convert_element_type.64, f32[128]{0:T(128)S(1)} %add_rsqrt_fusion), kind=kOutput, calls=%fused_computation.7 | convolution fusion | flops 338952192 | bytes 3727872 | tf_op jit(solution)/shard_map/dot_general | solution.py:332
  71.2 0.0 copy-done.3
  71.2 146.7 %shard_map.149 = bf16[8,40,4096]{2,1,0:T(8,128)(2,1)} custom-call(bf16[8,40,4096]{2,1,0:T(8,128)(2,1)} %bitcast.76, bf16[4096,384]{1,0:T(8,128)(2,1)} %bitcast.88, bf16[4096,384]{1,0:T(8,128)(2,1)} %bitcast.89, bf16[384,4096]{1,0:T(8,128)(2,1)} %bitcast.90), custom_call_target="tpu_custom_call" | custom-call | flops 12079595520 | bytes 41943040 | tf_op jit(solution)/shard_map/pallas_call | solution.py:245
  217.9 0.0 copy-start.1
  217.9 2.7 %convolution_multiply_fusion.1 = f32[128,4096]{1,0:T(8,128)S(1)} fusion(bf16[320,4096]{1,0:T(8,128)(2,1)} %bitcast.73, f32[128]{0:T(128)S(1)} %get-tuple-element.9, pred[128,2,320]{0,2,1:T(32,128)(4,1)S(1)} %get-tuple-element.10), kind=kOutput, calls=%fused_computation.10 | convolution fusion | flops 336068608 | bytes 4760064 | tf_op jit(solution)/shard_map/dot_general | solution.py:344
  220.6 0.0 copy-done.1
  220.6 1.7 fusion.8
  (10 shorter events, 0.1 us)
Async XLA Ops:
  7.2 4.3 %copy-start.8 = (s32[512,2]{0,1:T(2,128)S(1)}, s32[512,2]{0,1:T(2,128)}, u32[]{:S(2)}) copy-start(s32[512,2]{0,1:T(2,128)} %param.23) | copy-start | bytes 12292
  7.2 4.7 %copy-start.5 = (bf16[4096]{0:T(1024)(128)(2,1)S(1)}, bf16[4096]{0:T(1024)(128)(2,1)}, u32[]{:S(2)}) copy-start(bf16[4096]{0:T(1024)(128)(2,1)} %param.18) | copy-start | bytes 24580
  7.2 6.4 %copy-start.6 = (bf16[4096]{0:T(1024)(128)(2,1)S(1)}, bf16[4096]{0:T(1024)(128)(2,1)}, u32[]{:S(2)}) copy-start(bf16[4096]{0:T(1024)(128)(2,1)} %param.19) | copy-start | bytes 24580
  7.2 6.4 %copy-start.7 = (s32[128,2]{0,1:T(2,128)S(1)}, s32[128,2]{0,1:T(2,128)}, u32[]{:S(2)}) copy-start(s32[128,2]{0,1:T(2,128)} %param.24) | copy-start | bytes 3076
  7.2 6.4 %copy-start.2 = (bf16[128,4096]{1,0:T(8,128)(2,1)S(1)}, bf16[128,4096]{1,0:T(8,128)(2,1)}, u32[]{:S(2)}) copy-start(bf16[128,4096]{1,0:T(8,128)(2,1)} %param.14) | copy-start | bytes 3145732
  7.2 32.6 %all-gather.3.cloned.1.call-start = ((), (), s32[]{:S(2)}) async-start(), calls=%async_computation | async-start | bytes 3276800 | tf_op jit(solution)/shard_map/all_gather | solution.py:310
  43.7 1.5 copy-start.4
  53.1 3.2 %copy-start = (f32[8,512,128,4]{2,1,3,0:T(8,128)}, f32[8,512,128,4]{2,1,3,0:T(8,128)S(1)}, u32[]{:S(2)}) copy-start(f32[8,512,128,4]{2,1,3,0:T(8,128)S(1)} %fusion.21) | copy-start | bytes 25165828
  68.8 2.5 %copy-start.3 = (bf16[128,4096]{1,0:T(8,128)(2,1)}, bf16[128,4096]{1,0:T(8,128)(2,1)S(1)}, u32[]{:S(2)}) copy-start(bf16[128,4096]{1,0:T(8,128)(2,1)S(1)} %get-tuple-element.3) | copy-start | bytes 3145732
  217.9 2.7 %copy-start.1 = (bf16[8,40,4096]{2,1,0:T(8,128)(2,1)S(1)}, bf16[8,40,4096]{2,1,0:T(8,128)(2,1)}, u32[]{:S(2)}) copy-start(bf16[8,40,4096]{2,1,0:T(8,128)(2,1)} %shard_map.149) | copy-start | bytes 7864324
Sparse Core Ops, SparseCore 0:
  11.5 28.2 all-gather.2

commit v2 on v1

--- a/solution.py
+++ b/solution.py
@@ -60,6 +60,7 @@
 
 
 STEPS = 8
+AHEAD = 4
 
 
 def peer_mask(step):
@@ -151,7 +152,7 @@
         )
     pl.semaphore_wait(barrier, STEPS + 1)
 
-    for step in range(1, STEPS):
+    for step in range(1, AHEAD + 1):
         z_send(step).start()
     arrived[0, q_me] = outgoing[0]
 
@@ -179,6 +180,10 @@
             def _():
                 remote(Z, t, outgoing.at[t], arrived.at[t, q_me], peer(t), sp).wait_recv()
 
+                @pl.when(t < STEPS - AHEAD)
+                def _():
+                    z_send(t + AHEAD).start()
+
             x_send(t).start()
             core_send(t).start()
 
@@ -188,22 +193,9 @@
             remote(X, k, arrived.at[k, q_x], arrived.at[k, q_x], me, x_dev).wait_recv()
             core_forward(k).start()
 
-        @pl.when(t == 2)
-        def _():
-            for copy in weights:
-                copy.wait()
-
         @pl.when((t >= 2) & (t < STEPS + 2))
         def _():
             k = t - 2
-            remote(C1, k, arrived.at[k, q_core], arrived.at[k, q_core], me, core_dev).wait_recv()
-            remote(C2, k, arrived.at[k, q_diag], arrived.at[k, q_diag], me, core_dev).wait_recv()
-            compute(k)
-            part_send(k).start()
-
-        @pl.when((t >= 3) & (t < STEPS + 3))
-        def _():
-            k = t - 3
             part_send(k).wait_recv()
             part[k, q_x] = (
                 part[k, q_x].astype(jnp.float32)
@@ -211,9 +203,9 @@
             ).astype(jnp.bfloat16)
             x_part_send(k).start()
 
-        @pl.when(t >= 4)
-        def _():
-            k = t - 4
+        @pl.when(t >= 3)
+        def _():
+            k = t - 3
             x_part_send(k).wait_recv()
             part[k, q_me] = (
                 part[k, q_me].astype(jnp.float32)
@@ -225,9 +217,22 @@
             def _():
                 final_send(k).start()
 
+        @pl.when(t == 1)
+        def _():
+            for copy in weights:
+                copy.wait()
+
+        @pl.when((t >= 1) & (t < STEPS + 1))
+        def _():
+            k = t - 1
+            remote(C1, k, arrived.at[k, q_core], arrived.at[k, q_core], me, core_dev).wait_recv()
+            remote(C2, k, arrived.at[k, q_diag], arrived.at[k, q_diag], me, core_dev).wait_recv()
+            compute(k)
+            part_send(k).start()
+
         return carry
 
-    lax.fori_loop(0, STEPS + 4, body, 0)
+    lax.fori_loop(0, STEPS + 3, body, 0)
     returned[0] = part[0, q_me]
     for k in range(STEPS):
         if k > 0:

time: 232 us -> 228 us (0.983)
  Pallas kernels: 147 us -> 141 us
    pallas_call x1, Pallas kernels: 147 us -> 141 us  [expert_exchange(): pl.pallas_call(expert_kernel, out_shape=jax.ShapeDtypeStruct(outgoing.sha...]
where the time goes in v2:
time: 228 us; the launch traced here: 223 us
  Pallas kernels  141 us (62%)
  waiting for transfers between devices  25.2 us (11%)
  matrix products  21.3 us (9%)
  between operations  15 us (7%)
  local copies, waits for them, and re-layouts  14.1 us (6%)
  other arithmetic  6.85 us (3%)
    pallas_call x1, Pallas kernels, expert_exchange(): pl.pallas_call(expert_kernel, out_shape=jax.ShapeDtypeStruct(outgoing.sha...  141 us
    all_gather x1, waiting for transfers between devices, on_device(): shared = lax.all_gather(shared, 'sp', axis=0, tiled=False)  25.2 us
    dot_general x1, matrix products, attention_block(): jnp.einsum('hgqk,khd->qhgd', attn_probs, value_split, preferred_element_t...  9.83 us
  transfers between devices with their start and end apart: 1, of which 1 were waited for; matrix products, arithmetic and copies ran while one was open for 1% of the time, Pallas kernels for 0%

profile of v2, /device:TPU:0, one launch (start us, length us, event | category | flops | bytes accessed | tf_op | source)
XLA Modules:
  0.0 223.1 jit_solution(17916580184781038302)
XLA Ops:
  7.2 0.0 copy-start.8
  7.2 0.0 copy-start.5
  7.2 0.0 copy-start.6
  7.2 0.0 copy-start.7
  7.2 0.0 copy-start.2
  7.2 0.0 all-gather.3.cloned.1.call-start
  8.0 1.2 dynamic-slice_bitcast_fusion
  9.2 0.1 copy.43
  9.4 0.1 copy.44
  9.5 1.9 pad_maximum_fusion
  11.4 0.0 all-gather.3.cloned.1.call-update
  11.4 0.0 copy-done.8
  11.5 0.1 copy.51
  11.6 0.1 eq.44
  11.7 0.1 eq.40
  11.8 0.0 copy-done.5
  11.9 0.6 convert_element_type.55
  12.5 0.6 reduce-window.6
  13.0 0.2 slice_reduce_fusion
  13.3 0.1 fusion.36
  13.4 0.1 reduce_sum.50
  13.5 0.1 copy.53
  13.6 0.0 copy-done.6
  13.6 0.0 copy-done.7
  13.6 0.0 copy-done.2
  13.7 0.3 fusion.14
  13.9 0.6 add_rsqrt_fusion.1
  14.6 0.1 iota_compare_fusion
  14.6 25.2 %all-gather.3.cloned.1.call-done = bf16[1280,1024]{1,0:T(8,128)(2,1)} async-done(((bf16[320,1024]{1,0:T(8,128)(2,1)}), bf16[1280,1024]{1,0:T(8,128)(2,1)}) %all-gather.3.cloned.1.call-update) | async-done | bytes 2621456 | tf_op jit(solution)/shard_map/all_gather | solution.py:315
  39.8 1.1 slice.54
  40.9 2.8 %fusion.46 = (bf16[4,128,1024]{2,1,0:T(8,128)(2,1)S(1)}, bf16[4,128,1024]{2,1,0:T(8,128)(2,1)}) fusion(bf16[4,320,1024]{2,1,0:T(8,128)(2,1)} %bitcast.80), kind=kLoop, calls=%fused_computation.70 | loop fusion | bytes 4194304 | tf_op jit(solution)/shard_map/slice | solution.py:317
  43.7 0.0 copy-start.4
  43.7 0.4 copy.74
  44.1 0.2 fusion.47
  44.3 0.1 copy.65
  44.4 0.8 copy.66
  45.1 0.0 copy-done.4
  45.2 3.4 %fusion.7 = bf16[128,4096]{1,0:T(8,128)(2,1)} fusion(bf16[32,4096]{1,0:T(8,128)(2,1)} %bitcast.87, bf16[128,4096]{1,0:T(8,128)(2,1)S(1)} %copy-done.4, bf16[32,4096]{1,0:T(8,128)(2,1)S(1)} %bitcast.86, bf16[128,4096]{1,0:T(8,128)(2,1)S(1)} %copy-done.2, f32[4096]{0:T(1024)} %convert_element_type.55, f32[128]{0:T(128)} %add_rsqrt_fusion.1), kind=kOutput, calls=%fused_computation.12 | convolution fusion | flops 70782976 | bytes 3686912 | tf_op jit(solution)/shard_map/dot_general | solution.py:43
  48.5 1.8 reshape.95
  50.3 1.5 copy.64
  51.8 1.3 fusion.21
  53.1 0.0 copy-start
  53.1 2.2 fusion.48
  55.4 1.0 copy-done
  56.3 0.3 copy.63
  56.6 9.8 %fusion.10 = f32[8,128,4,128]{3,1,2,0:T(8,128)} fusion(f32[8,4,128]{2,1,0:T(4,128)S(1)} %fusion.48, bf16[512,8,128,1]{2,1,0,3:T(8,128)(2,1)S(1)} %bitcast.83, f32[8,512,128,4]{2,1,3,0:T(8,128)} %copy-done), kind=kOutput, calls=%fused_computation.15 | convolution fusion | flops 547361280 | bytes 11550720 | tf_op jit(solution)/shard_map/hgqk,khd->qhgd/dot_general | solution.py:56
  66.4 1.9 copy.50
  68.4 0.4 fusion.11
  68.8 0.0 copy-start.3
  68.8 2.4 %convolution_convert_fusion = bf16[320,4096]{1,0:T(8,128)(2,1)} fusion(pred[128,320]{0,1:T(8,128)(4,1)S(1)} %get-tuple-element.11, bf16[128,4096]{1,0:T(8,128)(2,1)S(1)} %get-tuple-element.3, f32[4096]{0:T(1024)S(1)} %convert_element_type.64, f32[128]{0:T(128)S(1)} %add_rsqrt_fusion), kind=kOutput, calls=%fused_computation.7 | convolution fusion | flops 338952192 | bytes 3727872 | tf_op jit(solution)/shard_map/dot_general | solution.py:337
  71.2 0.0 copy-done.3
  71.2 140.6 %shard_map.149 = bf16[8,40,4096]{2,1,0:T(8,128)(2,1)} custom-call(bf16[8,40,4096]{2,1,0:T(8,128)(2,1)} %bitcast.76, bf16[4096,384]{1,0:T(8,128)(2,1)} %bitcast.88, bf16[4096,384]{1,0:T(8,128)(2,1)} %bitcast.89, bf16[384,4096]{1,0:T(8,128)(2,1)} %bitcast.90), custom_call_target="tpu_custom_call" | custom-call | flops 12079595520 | bytes 41943040 | tf_op jit(solution)/shard_map/pallas_call | solution.py:250
  211.8 0.0 copy-start.1
  211.8 2.7 %convolution_multiply_fusion.1 = f32[128,4096]{1,0:T(8,128)S(1)} fusion(bf16[320,4096]{1,0:T(8,128)(2,1)} %bitcast.73, f32[128]{0:T(128)S(1)} %get-tuple-element.9, pred[128,2,320]{0,2,1:T(32,128)(4,1)S(1)} %get-tuple-element.10), kind=kOutput, calls=%fused_computation.10 | convolution fusion | flops 336068608 | bytes 4760064 | tf_op jit(solution)/shard_map/dot_general | solution.py:349
  214.5 0.0 copy-done.1
  214.5 1.7 fusion.8
  (10 shorter events, 0.1 us)
Async XLA Ops:
  7.2 4.3 %copy-start.8 = (s32[512,2]{0,1:T(2,128)S(1)}, s32[512,2]{0,1:T(2,128)}, u32[]{:S(2)}) copy-start(s32[512,2]{0,1:T(2,128)} %param.23) | copy-start | bytes 12292
  7.2 4.7 %copy-start.5 = (bf16[4096]{0:T(1024)(128)(2,1)S(1)}, bf16[4096]{0:T(1024)(128)(2,1)}, u32[]{:S(2)}) copy-start(bf16[4096]{0:T(1024)(128)(2,1)} %param.18) | copy-start | bytes 24580
  7.2 6.4 %copy-start.6 = (bf16[4096]{0:T(1024)(128)(2,1)S(1)}, bf16[4096]{0:T(1024)(128)(2,1)}, u32[]{:S(2)}) copy-start(bf16[4096]{0:T(1024)(128)(2,1)} %param.19) | copy-start | bytes 24580
  7.2 6.4 %copy-start.7 = (s32[128,2]{0,1:T(2,128)S(1)}, s32[128,2]{0,1:T(2,128)}, u32[]{:S(2)}) copy-start(s32[128,2]{0,1:T(2,128)} %param.24) | copy-start | bytes 3076
  7.2 6.4 %copy-start.2 = (bf16[128,4096]{1,0:T(8,128)(2,1)S(1)}, bf16[128,4096]{1,0:T(8,128)(2,1)}, u32[]{:S(2)}) copy-start(bf16[128,4096]{1,0:T(8,128)(2,1)} %param.14) | copy-start | bytes 3145732
  7.2 32.6 %all-gather.3.cloned.1.call-start = ((), (), s32[]{:S(2)}) async-start(), calls=%async_computation | async-start | bytes 3276800 | tf_op jit(solution)/shard_map/all_gather | solution.py:315
  43.7 1.5 copy-start.4
  53.1 3.2 %copy-start = (f32[8,512,128,4]{2,1,3,0:T(8,128)}, f32[8,512,128,4]{2,1,3,0:T(8,128)S(1)}, u32[]{:S(2)}) copy-start(f32[8,512,128,4]{2,1,3,0:T(8,128)S(1)} %fusion.21) | copy-start | bytes 25165828
  68.8 2.5 %copy-start.3 = (bf16[128,4096]{1,0:T(8,128)(2,1)}, bf16[128,4096]{1,0:T(8,128)(2,1)S(1)}, u32[]{:S(2)}) copy-start(bf16[128,4096]{1,0:T(8,128)(2,1)S(1)} %get-tuple-element.3) | copy-start | bytes 3145732
  211.8 2.7 %copy-start.1 = (bf16[8,40,4096]{2,1,0:T(8,128)(2,1)S(1)}, bf16[8,40,4096]{2,1,0:T(8,128)(2,1)}, u32[]{:S(2)}) copy-start(bf16[8,40,4096]{2,1,0:T(8,128)(2,1)} %shard_map.149) | copy-start | bytes 7864324
Sparse Core Ops, SparseCore 0:
  11.5 28.2 all-gather.2

commit v3 on v2

--- a/solution.py
+++ b/solution.py
@@ -64,7 +64,8 @@
 
 
 def peer_mask(step):
-    return (step * 2) % STEPS + step // 4
+    middle, last = (step // 2) % 2, step // 4
+    return step % 2 + 2 * last + 4 * ((middle + last) % 2)
 
 
 def xor3(a, b):
@@ -328,7 +329,8 @@
     flat_routes, slot_index = route_slots(own_routes, experts)
     if in_kernel:
         mask = flat_routes ^ lax.axis_index("ep")
-        flat_routes = mask // 2 + (mask % 2) * 4
+        near, far = (mask // 2) % 2, mask // 4
+        flat_routes = mask % 2 + 4 * near + 2 * ((far + near) % 2)
     position = (flat_routes * capacity + slot_index).reshape(tokens_dev, top_count)
     slots = jnp.arange(experts * capacity, dtype=jnp.int32)
     chosen = position[:, :, None] == slots

time: 228 us -> 235 us (1.031); the launches traced: 223 us -> 235 us
  Pallas kernels: 141 us -> 152 us
    pallas_call x1, Pallas kernels: 141 us -> 152 us  [expert_exchange(): pl.pallas_call(expert_kernel, out_shape=jax.ShapeDtypeStruct(outgoing.sha...]
  transfers between devices with their start and end apart: 1 -> 1, of which waited for: 1 -> 1; matrix products, arithmetic and copies ran while one was open for 1% -> 2% of each run, Pallas kernels for 0% -> 0%
where the time goes in v3:
time: 235 us
  Pallas kernels  152 us (65%)
  waiting for transfers between devices  24.6 us (10%)
  matrix products  21.3 us (9%)
  between operations  15 us (6%)
  local copies, waits for them, and re-layouts  14.9 us (6%)
  other arithmetic  6.92 us (3%)
    pallas_call x1, Pallas kernels, expert_exchange(): pl.pallas_call(expert_kernel, out_shape=jax.ShapeDtypeStruct(outgoing.sha...  152 us
    all_gather x1, waiting for transfers between devices, on_device(): shared = lax.all_gather(shared, 'sp', axis=0, tiled=False)  24.6 us
    dot_general x1, matrix products, attention_block(): jnp.einsum('hgqk,khd->qhgd', attn_probs, value_split, preferred_element_t...  9.83 us
  transfers between devices with their start and end apart: 1, of which 1 were waited for; matrix products, arithmetic and copies ran while one was open for 2% of the time, Pallas kernels for 0%

profile of v3, /device:TPU:0, one launch (start us, length us, event | category | flops | bytes accessed | tf_op | source)
XLA Modules:
  0.0 235.0 jit_solution(6037915580020728366)
XLA Ops:
  7.2 0.0 copy-start
  7.2 0.0 copy-start.7
  7.2 0.0 copy-start.8
  7.2 0.0 copy-start.10
  7.2 0.0 copy-start.3
  7.2 0.0 all-gather.3.cloned.1.call-start
  8.0 1.2 dynamic-slice_bitcast_fusion
  9.2 0.1 copy.33
  9.4 0.1 copy.34
  9.5 1.9 pad_maximum_fusion
  11.4 0.0 all-gather.3.cloned.1.call-update
  11.5 0.0 copy-done
  11.5 0.1 copy.52
  11.6 0.1 eq.46
  11.7 0.1 eq.42
  11.9 0.0 copy-done.7
  11.9 0.6 reduce-window.6
  12.5 0.2 slice_reduce_fusion
  12.8 0.1 fusion.47
  12.9 0.1 reduce_sum.50
  13.0 0.2 fusion.34
  13.2 0.1 copy.42
  13.2 0.0 copy-done.8
  13.2 0.6 convert_element_type.64
  13.9 0.0 copy-done.10
  13.9 0.0 copy-done.3
  13.9 0.3 fusion.14
  14.2 0.5 add_rsqrt_fusion.1
  14.7 0.5 slice_bitcast_fusion.4
  15.2 0.1 iota_compare_fusion
  15.3 24.6 %all-gather.3.cloned.1.call-done = bf16[1280,1024]{1,0:T(8,128)(2,1)} async-done(((bf16[320,1024]{1,0:T(8,128)(2,1)}), bf16[1280,1024]{1,0:T(8,128)(2,1)}) %all-gather.3.cloned.1.call-update) | async-done | bytes 2621456 | tf_op jit(solution)/shard_map/all_gather | solution.py:316
  39.9 1.1 slice.54
  40.9 2.8 %fusion.55 = (bf16[4,128,1024]{2,1,0:T(8,128)(2,1)S(1)}, bf16[4,128,1024]{2,1,0:T(8,128)(2,1)}) fusion(bf16[4,320,1024]{2,1,0:T(8,128)(2,1)} %bitcast.80), kind=kLoop, calls=%fused_computation.88 | loop fusion | bytes 4194304 | tf_op jit(solution)/shard_map/slice | solution.py:318
  43.7 0.0 copy-start.5
  43.7 0.4 copy.64
  44.1 0.2 fusion.56
  44.3 0.1 copy.55
  44.4 0.8 copy.56
  45.2 0.0 copy-done.5
  45.2 3.4 %fusion.7 = bf16[128,4096]{1,0:T(8,128)(2,1)} fusion(bf16[32,4096]{1,0:T(8,128)(2,1)} %bitcast.87, bf16[128,4096]{1,0:T(8,128)(2,1)S(1)} %copy-done.5, bf16[32,4096]{1,0:T(8,128)(2,1)S(1)} %bitcast.86, bf16[128,4096]{1,0:T(8,128)(2,1)S(1)} %copy-done.3, f32[4096]{0:T(1024)S(1)} %convert_element_type.55, f32[128]{0:T(128)} %add_rsqrt_fusion.1), kind=kOutput, calls=%fused_computation.12 | convolution fusion | flops 70782976 | bytes 3686912 | tf_op jit(solution)/shard_map/dot_general | solution.py:43
  48.6 1.8 reshape.130
  50.4 1.5 copy.54
  51.9 1.3 fusion.21
  53.1 0.0 copy-start.1
  53.1 2.2 fusion.57
  55.3 1.1 copy-done.1
  56.4 0.3 copy.53
  56.6 9.8 %fusion.10 = f32[8,128,4,128]{3,1,2,0:T(8,128)} fusion(f32[8,4,128]{2,1,0:T(4,128)S(1)} %fusion.57, bf16[512,8,128,1]{2,1,0,3:T(8,128)(2,1)S(1)} %bitcast.83, f32[8,512,128,4]{2,1,3,0:T(8,128)} %copy-done.1), kind=kOutput, calls=%fused_computation.15 | convolution fusion | flops 547361280 | bytes 11550720 | tf_op jit(solution)/shard_map/hgqk,khd->qhgd/dot_general | solution.py:56
  66.5 1.9 copy.40
  68.4 0.0 copy-start.6
  68.4 0.4 fusion.11
  68.8 0.0 copy-start.4
  68.8 0.3 copy-done.6
  69.1 2.5 %convolution_convert_fusion = bf16[320,4096]{1,0:T(8,128)(2,1)} fusion(pred[128,320]{0,1:T(8,128)(4,1)S(1)} %get-tuple-element.11, bf16[128,4096]{1,0:T(8,128)(2,1)S(1)} %get-tuple-element.3, f32[4096]{0:T(1024)S(1)} %copy-done.6, f32[128]{0:T(128)S(1)} %add_rsqrt_fusion), kind=kOutput, calls=%fused_computation.7 | convolution fusion | flops 338952192 | bytes 3727872 | tf_op jit(solution)/shard_map/dot_general | solution.py:339
  71.6 0.0 copy-done.4
  71.6 0.0 copy-start.9
  71.6 152.1 %shard_map.149 = bf16[8,40,4096]{2,1,0:T(8,128)(2,1)} custom-call(bf16[8,40,4096]{2,1,0:T(8,128)(2,1)} %bitcast.76, bf16[4096,384]{1,0:T(8,128)(2,1)} %bitcast.88, bf16[4096,384]{1,0:T(8,128)(2,1)} %bitcast.89, bf16[384,4096]{1,0:T(8,128)(2,1)} %bitcast.90), custom_call_target="tpu_custom_call" | custom-call | flops 12079595520 | bytes 41943040 | tf_op jit(solution)/shard_map/pallas_call | solution.py:251
  223.7 0.0 copy-start.2
  223.7 0.0 copy-done.9
  223.7 2.7 %convolution_multiply_fusion.1 = f32[128,4096]{1,0:T(8,128)S(1)} fusion(bf16[320,4096]{1,0:T(8,128)(2,1)} %bitcast.73, f32[128]{0:T(128)S(1)} %copy-done.9, pred[128,2,320]{0,2,1:T(32,128)(4,1)S(1)} %get-tuple-element.10), kind=kOutput, calls=%fused_computation.10 | convolution fusion | flops 336068608 | bytes 4760064 | tf_op jit(solution)/shard_map/dot_general | solution.py:351
  226.4 0.0 copy-done.2
  226.4 1.7 fusion.8
  (8 shorter events, 0.1 us)
Async XLA Ops:
  7.2 4.3 %copy-start = (s32[512,2]{0,1:T(2,128)S(1)}, s32[512,2]{0,1:T(2,128)}, u32[]{:S(2)}) copy-start(s32[512,2]{0,1:T(2,128)} %param.23) | copy-start | bytes 12292
  7.2 4.7 %copy-start.7 = (bf16[4096]{0:T(1024)(128)(2,1)S(1)}, bf16[4096]{0:T(1024)(128)(2,1)}, u32[]{:S(2)}) copy-start(bf16[4096]{0:T(1024)(128)(2,1)} %param.18) | copy-start | bytes 24580
  7.2 6.0 %copy-start.8 = (bf16[4096]{0:T(1024)(128)(2,1)S(1)}, bf16[4096]{0:T(1024)(128)(2,1)}, u32[]{:S(2)}) copy-start(bf16[4096]{0:T(1024)(128)(2,1)} %param.19) | copy-start | bytes 24580
  7.2 6.7 %copy-start.10 = (s32[128,2]{0,1:T(2,128)S(1)}, s32[128,2]{0,1:T(2,128)}, u32[]{:S(2)}) copy-start(s32[128,2]{0,1:T(2,128)} %param.24) | copy-start | bytes 3076
  7.2 6.7 %copy-start.3 = (bf16[128,4096]{1,0:T(8,128)(2,1)S(1)}, bf16[128,4096]{1,0:T(8,128)(2,1)}, u32[]{:S(2)}) copy-start(bf16[128,4096]{1,0:T(8,128)(2,1)} %param.14) | copy-start | bytes 3145732
  7.2 32.6 %all-gather.3.cloned.1.call-start = ((), (), s32[]{:S(2)}) async-start(), calls=%async_computation | async-start | bytes 3276800 | tf_op jit(solution)/shard_map/all_gather | solution.py:316
  43.7 1.5 copy-start.5
  53.1 3.2 %copy-start.1 = (f32[8,512,128,4]{2,1,3,0:T(8,128)}, f32[8,512,128,4]{2,1,3,0:T(8,128)S(1)}, u32[]{:S(2)}) copy-start(f32[8,512,128,4]{2,1,3,0:T(8,128)S(1)} %fusion.21) | copy-start | bytes 25165828
  68.4 0.7 copy-start.6
  68.8 2.8 %copy-start.4 = (bf16[128,4096]{1,0:T(8,128)(2,1)}, bf16[128,4096]{1,0:T(8,128)(2,1)S(1)}, u32[]{:S(2)}) copy-start(bf16[128,4096]{1,0:T(8,128)(2,1)S(1)} %get-tuple-element.3) | copy-start | bytes 3145732
  71.6 152.1 %copy-start.9 = (f32[128]{0:T(128)S(1)}, f32[128]{0:T(128)}, u32[]{:S(2)}) copy-start(f32[128]{0:T(128)} %get-tuple-element.9) | copy-start | bytes 1540
  223.7 2.7 %copy-start.2 = (bf16[8,40,4096]{2,1,0:T(8,128)(2,1)S(1)}, bf16[8,40,4096]{2,1,0:T(8,128)(2,1)}, u32[]{:S(2)}) copy-start(bf16[8,40,4096]{2,1,0:T(8,128)(2,1)} %shard_map.149) | copy-start | bytes 7864324
Sparse Core Ops, SparseCore 0:
  11.6 28.2 all-gather.2
